TPU v7x, 32 devices: a whole 2x2x4 slice. The times are simulated.
32 devices in a mesh: src: 8 (over y, x, core), tgt: 4 (over z).
Axes of the slice: x: 2, y: 2, z: 4, core: 2. Of those that a mesh axis runs over, the one named last changes fastest.
Arguments:
- feat_in: bfloat16 [32, 49, 128], P(('src', 'tgt')), may hold values from -6 to 6
- ffn_in: bfloat16 [32, 49, 128], P(('src', 'tgt')), may hold values from -6 to 6
- grad_out: bfloat16 [32, 49, 128], P(('src', 'tgt')), may hold values from -6 to 6
- ffn_up: bfloat16 [128, 512], replicated, may hold values from -0.5 to 0.5
- ffn_down: bfloat16 [512, 128], replicated, may hold values from -0.25 to 0.25
- so2_zero: bfloat16 [896, 1024], P('tgt'), may hold values from -0.1875 to 0.1875
- so2_one: bfloat16 [2, 768, 768], P(None, 'tgt'), may hold values from -0.15625 to 0.15625
- so2_two: bfloat16 [2, 640, 640], P(None, 'tgt'), may hold values from -0.15625 to 0.15625
- wigner: bfloat16 [64, 29, 49], replicated, may hold values from -1 to 1
- edge_src: int32 [8, 4, 128], P('src', 'tgt'), may hold values from 0 to 3
- edge_tgt: int32 [8, 4, 128], P('src', 'tgt'), may hold values from 0 to 7
- edge_angle: int32 [8, 4, 128], P('src', 'tgt'), may hold values from 0 to 63
- edge_radial: bfloat16 [8, 4, 128, 128], P('src', 'tgt'), may hold values from 0.25 to 2
- edge_count: int32 [8, 4], P('src', 'tgt'), may hold values from 1 to 128, as said below
Outputs:
- feat_grad: bfloat16 [32, 49, 128], P(('src', 'tgt'))
Inputs may be any that keep to these rules, and one draw needn't show every extreme that they name: The slots of a block at or past its edge_count are padding. Some block holds 128 edges.
All inputs are finite; a program needn't handle non-finite values.
Results may differ from a plain program's by a relative error of at most 0.006.
Values may be sent and summed in bfloat16 or wider, within the bound.
A program may use at most 64 MiB of HBM per device.

v0:
```python
import math

import jax
import jax.numpy as jnp
import numpy as np
from jax import lax
from jax.sharding import PartitionSpec as P

LMAX = 6
GRID_SIDE = 14


message_scale = 0.125


def sphere_tables(degree_max, grid_side):
    polar_angle = (np.arange(grid_side) + 0.5) * np.pi / grid_side
    azimuth = np.arange(grid_side) * 2.0 * np.pi / grid_side
    cosine = np.cos(polar_angle)
    sine_theta = np.sin(polar_angle)
    coef_count = (degree_max + 1) * (degree_max + 1)
    harmonics = np.zeros((grid_side, grid_side, coef_count))
    for order_m in range(degree_max + 1):
        diagonal = np.ones(grid_side)
        for factor in range(1, order_m + 1):
            diagonal = diagonal * (2 * factor - 1) * sine_theta
        legendre = {order_m: diagonal}
        if order_m + 1 <= degree_max:
            legendre[order_m + 1] = cosine * (2 * order_m + 1) * diagonal
        for degree in range(order_m + 2, degree_max + 1):
            legendre[degree] = (
                (2 * degree - 1) * cosine * legendre[degree - 1]
                - (degree + order_m - 1) * legendre[degree - 2]
            ) / (degree - order_m)
        for degree in range(order_m, degree_max + 1):
            scaling = math.sqrt(
                (2 * degree + 1)
                / (4.0 * math.pi)
                * math.factorial(degree - order_m)
                / math.factorial(degree + order_m)
            )
            if order_m > 0:
                scaling = scaling * math.sqrt(2.0)
            polar_part = scaling * legendre[degree]
            centre = degree * degree + degree
            harmonics[:, :, centre + order_m] = (
                polar_part[:, None] * np.cos(order_m * azimuth)[None, :]
            )
            if order_m > 0:
                harmonics[:, :, centre - order_m] = (
                    polar_part[:, None] * np.sin(order_m * azimuth)[None, :]
                )
    to_grid = harmonics.reshape(grid_side * grid_side, coef_count)
    quadrature = np.repeat(sine_theta * (np.pi / grid_side) * (2.0 * np.pi / grid_side), grid_side)
    from_grid = (to_grid * quadrature[:, None]).T
    return (
        jnp.asarray(to_grid, jnp.float32).astype(jnp.bfloat16),
        jnp.asarray(from_grid, jnp.float32).astype(jnp.bfloat16),
    )


def matmul_plain(left, right):
    return jnp.dot(left, right, preferred_element_type=jnp.float32)


def matmul_flip(left, right):
    return lax.dot_general(
        left, right, (((1,), (1,)), ((), ())), preferred_element_type=jnp.float32
    )


def ffn_backward(ffn_rows, grad_rows, ffn_up, ffn_down, to_grid, from_grid):
    atom_count, coef_count, channels = ffn_rows.shape
    grid_feat = jnp.einsum(
        "pk,akc->apc", to_grid, ffn_rows, preferred_element_type=jnp.float32
    ).astype(jnp.bfloat16)
    grid_points = grid_feat.shape[1]
    pre_act = matmul_plain(grid_feat.reshape(atom_count * grid_points, channels), ffn_up)
    grad_value = jnp.einsum(
        "kp,akc->apc", from_grid, grad_rows, preferred_element_type=jnp.float32
    ).astype(jnp.bfloat16)
    grad_act = matmul_flip(grad_value.reshape(atom_count * grid_points, channels), ffn_down)
    sigmoid_pre = jax.nn.sigmoid(pre_act)
    grad_pre = (grad_act * sigmoid_pre * (1.0 + pre_act * (1.0 - sigmoid_pre))).astype(jnp.bfloat16)
    grad_grid = matmul_flip(grad_pre, ffn_up).astype(jnp.bfloat16)
    ffn_term = jnp.einsum(
        "pk,apc->akc",
        to_grid,
        grad_grid.reshape(atom_count, grid_points, channels),
        preferred_element_type=jnp.float32,
    )
    return (grad_rows.astype(jnp.float32) + ffn_term).astype(jnp.bfloat16)


def so2_higher(rotated, w_one, w_two, degree_max, channels):
    cut_a = (degree_max + 1) * channels
    cut_b = cut_a + degree_max * channels
    cut_c = cut_b + degree_max * channels
    cut_d = cut_c + (degree_max - 1) * channels
    one_plus = rotated[:, cut_a:cut_b]
    one_minus = rotated[:, cut_b:cut_c]
    two_plus = rotated[:, cut_c:cut_d]
    two_minus = rotated[:, cut_d:]
    out_one_plus = matmul_plain(one_plus, w_one[0]) - matmul_plain(one_minus, w_one[1])
    out_one_minus = matmul_plain(one_minus, w_one[0]) + matmul_plain(one_plus, w_one[1])
    out_two_plus = matmul_plain(two_plus, w_two[0]) - matmul_plain(two_minus, w_two[1])
    out_two_minus = matmul_plain(two_minus, w_two[0]) + matmul_plain(two_plus, w_two[1])
    return jnp.concatenate([out_one_plus, out_one_minus, out_two_plus, out_two_minus], axis=1)


def so2_forward(rotated, weights, degree_max, channels):
    w_zero, w_one, w_two = weights
    cut_a = (degree_max + 1) * channels
    out_zero = matmul_plain(rotated[:, :cut_a], w_zero)
    return jnp.concatenate(
        [out_zero, so2_higher(rotated, w_one, w_two, degree_max, channels)], axis=1
    )


def so2_backward(grad_pre, weights, degree_max, channels):
    w_zero, w_one, w_two = weights
    cut_a = (degree_max + 2) * channels
    cut_b = cut_a + degree_max * channels
    cut_c = cut_b + degree_max * channels
    cut_d = cut_c + (degree_max - 1) * channels
    grad_zero = grad_pre[:, :cut_a]
    grad_one_plus = grad_pre[:, cut_a:cut_b]
    grad_one_minus = grad_pre[:, cut_b:cut_c]
    grad_two_plus = grad_pre[:, cut_c:cut_d]
    grad_two_minus = grad_pre[:, cut_d:]
    back_zero = matmul_flip(grad_zero, w_zero)
    back_one_plus = matmul_flip(grad_one_plus, w_one[0]) + matmul_flip(grad_one_minus, w_one[1])
    back_one_minus = matmul_flip(grad_one_minus, w_one[0]) - matmul_flip(grad_one_plus, w_one[1])
    back_two_plus = matmul_flip(grad_two_plus, w_two[0]) + matmul_flip(grad_two_minus, w_two[1])
    back_two_minus = matmul_flip(grad_two_minus, w_two[0]) - matmul_flip(grad_two_plus, w_two[1])
    return jnp.concatenate(
        [back_zero, back_one_plus, back_one_minus, back_two_plus, back_two_minus], axis=1
    )


def gate_backward(hidden, grad_o, degree_max):
    gate_index = degree_max + 1
    scalar_pre = hidden[:, 0]
    gate_pre = hidden[:, gate_index]
    sigmoid_gate = jax.nn.sigmoid(gate_pre)
    sigmoid_scalar = jax.nn.sigmoid(scalar_pre)
    grad_scalar = grad_o[:, 0] * sigmoid_scalar * (1.0 + scalar_pre * (1.0 - sigmoid_scalar))
    gated_rows = jnp.concatenate([hidden[:, 1:gate_index], hidden[:, gate_index + 1 :]], axis=1)
    grad_rows = grad_o[:, 1:]
    grad_gate = jnp.sum(grad_rows * gated_rows, axis=1) * sigmoid_gate * (1.0 - sigmoid_gate)
    grad_gated = grad_rows * sigmoid_gate[:, None, :]
    return jnp.concatenate(
        [
            grad_scalar[:, None],
            grad_gated[:, :degree_max],
            grad_gate[:, None],
            grad_gated[:, degree_max:],
        ],
        axis=1,
    )


def on_device(
    feat_in,
    ffn_in,
    grad_out,
    ffn_up,
    ffn_down,
    so2_zero,
    so2_one,
    so2_two,
    wigner,
    edge_src,
    edge_tgt,
    edge_angle,
    edge_radial,
    edge_count,
):
    atom_count, coef_count, channels = feat_in.shape
    angle_bins, kept_rows = (wigner.shape[0], wigner.shape[1])
    slot_total = edge_src.shape[2]
    block_rows = min(128, slot_total)
    to_grid, from_grid = sphere_tables(LMAX, GRID_SIDE)
    source_all = lax.all_gather(feat_in, "tgt", axis=0, tiled=True)
    source_count = source_all.shape[0]
    source_flat = source_all.reshape(source_count, coef_count * channels)
    forward_weights = (
        lax.all_gather(so2_zero, "tgt", axis=0, tiled=True),
        lax.all_gather(so2_one, "tgt", axis=1, tiled=True),
        lax.all_gather(so2_two, "tgt", axis=1, tiled=True),
    )
    target_grad = ffn_backward(ffn_in, grad_out, ffn_up, ffn_down, to_grid, from_grid)
    target_all = lax.all_gather(target_grad, "src", axis=0, tiled=True)
    target_count = target_all.shape[0]
    target_flat = target_all.reshape(target_count, coef_count * channels)
    wigner_flat = wigner.reshape(angle_bins, kept_rows * coef_count)
    src_slots = edge_src.reshape(slot_total)
    tgt_slots = edge_tgt.reshape(slot_total)
    angle_slots = edge_angle.reshape(slot_total)
    radial_slots = edge_radial.reshape(slot_total, channels)
    live_count = edge_count.reshape(())
    source_labels = jnp.arange(source_count, dtype=jnp.int32)
    target_labels = jnp.arange(target_count, dtype=jnp.int32)
    angle_labels = jnp.arange(angle_bins, dtype=jnp.int32)
    block_count = slot_total // block_rows

    def rotate_block():
        pick_source = (src_slots[:, None] == source_labels[None, :]).astype(jnp.bfloat16)
        source_rows = (
            matmul_plain(pick_source, source_flat)
            .astype(jnp.bfloat16)
            .reshape(block_rows, coef_count, channels)
        )
        pick_angle = (angle_slots[:, None] == angle_labels[None, :]).astype(jnp.bfloat16)
        rotation = (
            matmul_plain(pick_angle, wigner_flat)
            .astype(jnp.bfloat16)
            .reshape(block_rows, kept_rows, coef_count)
        )
        rotated = jnp.einsum(
            "erk,ekc->erc", rotation, source_rows, preferred_element_type=jnp.float32
        ).astype(jnp.bfloat16)
        return (rotated.reshape(block_rows, kept_rows * channels), rotation)

    def forward_step(block_index, buffers):
        first_slot = block_index * block_rows
        rotated, rotation = rotate_block()
        hidden = so2_forward(rotated, forward_weights, LMAX, channels)
        hidden = (
            hidden.reshape(block_rows, kept_rows + 1, channels)
            * radial_slots.astype(jnp.float32)[:, None, :]
        )
        hidden_all = hidden.reshape(block_rows, (kept_rows + 1) * channels)
        return (hidden_all, rotation)

    hidden_all, rotation_all = lax.fori_loop(
        0,
        block_count,
        forward_step,
        (
            jnp.zeros((slot_total, (kept_rows + 1) * channels), jnp.float32),
            jnp.zeros((slot_total, kept_rows, coef_count), jnp.bfloat16),
        ),
    )

    def backward_step(block_index, partial_value):
        first_slot = block_index * block_rows
        radial = radial_slots.astype(jnp.float32)
        pick_target = (tgt_slots[:, None] == target_labels[None, :]).astype(jnp.bfloat16)
        target_rows = (
            matmul_plain(pick_target, target_flat)
            .astype(jnp.bfloat16)
            .reshape(block_rows, coef_count, channels)
        )
        hidden = hidden_all.reshape(block_rows, kept_rows + 1, channels)
        grad_o = (
            jnp.einsum(
                "erk,ekc->erc", rotation_all, target_rows, preferred_element_type=jnp.float32
            )
            * message_scale
        )
        grad_hidden = gate_backward(hidden, grad_o, LMAX)
        grad_pre = (
            (grad_hidden * radial[:, None, :])
            .astype(jnp.bfloat16)
            .reshape(block_rows, (kept_rows + 1) * channels)
        )
        grad_rot = (
            so2_backward(grad_pre, forward_weights, LMAX, channels)
            .astype(jnp.bfloat16)
            .reshape(block_rows, kept_rows, channels)
        )
        grad_edge = jnp.einsum(
            "erk,erc->ekc", rotation_all, grad_rot, preferred_element_type=jnp.float32
        ).astype(jnp.bfloat16)
        live_slot = first_slot + jnp.arange(block_rows, dtype=jnp.int32) < live_count
        pick_back = ((src_slots[:, None] == source_labels[None, :]) & live_slot[:, None]).astype(
            jnp.bfloat16
        )
        return partial_value + lax.dot_general(
            pick_back,
            grad_edge.reshape(block_rows, coef_count * channels),
            (((0,), (0,)), ((), ())),
            preferred_element_type=jnp.float32,
        )

    partial_value = lax.fori_loop(
        0, block_count, backward_step, jnp.zeros((source_count, coef_count * channels), jnp.float32)
    )
    summed = lax.psum_scatter(
        partial_value.reshape(source_count, coef_count, channels),
        "tgt",
        scatter_dimension=0,
        tiled=True,
    )
    return (target_grad.astype(jnp.float32) + summed).astype(jnp.bfloat16)


def solution(mesh):
    placed = (
        P(("src", "tgt"), None, None),
        P(("src", "tgt"), None, None),
        P(("src", "tgt"), None, None),
        P(),
        P(),
        P("tgt", None),
        P(None, "tgt", None),
        P(None, "tgt", None),
        P(),
        P("src", "tgt", None),
        P("src", "tgt", None),
        P("src", "tgt", None),
        P("src", "tgt", None, None),
        P("src", "tgt"),
    )
    return jax.shard_map(
        on_device,
        mesh=mesh,
        in_specs=placed,
        out_specs=P(("src", "tgt"), None, None),
        check_vma=False,
    )
```

profile of v0, /device:TPU:0, one launch (start us, length us, event | category | flops | bytes accessed | tf_op | source)
XLA Modules:
  0.0 213.3 jit_solution(14417183649635416894)
XLA Ops:
  6.5 0.7 all-gather.8.cloned.1.call-update
  7.3 0.7 all-gather.4.cloned.1.call-update
  8.1 0.7 all-gather.6.cloned.1.call-update
  8.8 2.0 copy.70
  10.8 0.7 reshape.94
  12.1 1.7 copy.83
  15.0 10.7 %all_gather.15 = bf16[8,49,128]{2,1,0:T(8,128)(2,1)S(1)} all-gather(bf16[1,49,128]{2,1,0:T(8,128)(2,1)S(1)} %fusion.23), channel_id=1, replica_groups=mesh['src'=8,'tgt'=4] {'src'}, dimensions={0}, use_global_device_ids=true | all-gather | bytes 112896 | tf_op jit(solution)/shard_map/all_gather | solution.py:193
  26.3 2.2 %copy.71 = bf16[128,6272]{0,1:T(8,128)(2,1)} copy(bf16[128,6272]{1,0:T(8,128)(2,1)S(1)} %convolution_convert_fusion.1) | data formatting | bytes 3211264 | tf_op jit(solution)/shard_map/while/body/eval_jaxpr/convert_element_type | solution.py:252
  28.5 2.9 %copy.73 = bf16[128,49,128]{2,1,0:T(8,128)(2,1)S(1)} copy(bf16[128,49,128]{0,2,1:T(8,128)(2,1)} %bitcast.107) | data formatting | bytes 3211264 | tf_op jit(solution)/shard_map/while/body/eval_jaxpr/reshape | solution.py:253
  31.4 14.0 %all_gather.16 = bf16[4,49,128]{2,1,0:T(8,128)(2,1)S(1)} all-gather(bf16[1,49,128]{2,1,0:T(8,128)(2,1)S(1)} %copy-done.13), channel_id=1, replica_groups=mesh['src'=8,'tgt'=4] {'tgt'}, dimensions={0}, use_global_device_ids=true | all-gather | bytes 62720 | tf_op jit(solution)/shard_map/all_gather | solution.py:184
  45.4 1.8 convolution_convert_fusion
  47.2 3.7 %copy.75 = bf16[128,6272]{0,1:T(8,128)(2,1)} copy(bf16[128,6272]{1,0:T(8,128)(2,1)} %convolution_convert_fusion) | data formatting | bytes 3211264 | tf_op jit(solution)/shard_map/while/body/eval_jaxpr/convert_element_type | solution.py:211
  50.9 3.5 %copy.77 = bf16[128,49,128]{2,1,0:T(8,128)(2,1)} copy(bf16[128,49,128]{0,2,1:T(8,128)(2,1)} %bitcast.108) | data formatting | bytes 3211264 | tf_op jit(solution)/shard_map/while/body/eval_jaxpr/reshape | solution.py:212
  54.4 3.1 %convolution_convert_fusion.4 = bf16[128,29,128]{2,1,0:T(8,128)(2,1)} fusion(bf16[128,29,49]{2,1,0:T(8,128)(2,1)S(1)} %copy.83, bf16[128,49,128]{2,1,0:T(8,128)(2,1)} %copy.77), kind=kOutput, calls=%fused_computation.12 | convolution fusion | flops 47038464 | bytes 2919680 | tf_op jit(solution)/shard_map/while/body/eval_jaxpr/erk,ekc->erc/dot_general | solution.py:220
  57.5 2.7 %copy.78 = bf16[128,29,128]{0,2,1:T(8,128)(2,1)} copy(bf16[128,29,128]{2,1,0:T(8,128)(2,1)} %convolution_convert_fusion.4) | data formatting | bytes 1900544 | tf_op jit(solution)/shard_map/while/body/eval_jaxpr/convert_element_type | solution.py:222
  61.4 0.6 fusion.80
  62.0 2.5 %copy_multiply_fusion = f32[128,29,128]{2,0,1:T(8,128)} fusion(f32[128,29,128]{2,1,0:T(8,128)S(1)} %fusion.80), kind=kLoop, calls=%fused_computation.5 | loop fusion | flops 475136 | bytes 3801088 | tf_op jit(solution)/shard_map/while/body/eval_jaxpr/mul | solution.py:257
  64.6 1.5 fusion.31
  66.0 1.5 fusion.30
  67.5 25.1 %all-gather.4.cloned.1.call-done = bf16[896,1024]{1,0:T(8,128)(2,1)} async-done(((bf16[224,1024]{1,0:T(8,128)(2,1)}), bf16[896,1024]{1,0:T(8,128)(2,1)}) %all-gather.4.cloned.1.call-update) | async-done | bytes 1835024 | tf_op jit(solution)/shard_map/all_gather | solution.py:188
  92.6 2.8 %convolution_dynamic-update-slice_fusion = f32[128,3840]{1,0:T(8,128)} fusion(bf16[896,1024]{1,0:T(8,128)(2,1)} %all-gather.4.cloned.1.call-done, bf16[128,3712]{0,1:T(8,128)(2,1)S(1)} %bitcast.100), kind=kOutput, calls=%fused_computation.13 | convolution fusion | flops 234881024 | bytes 2588672 | tf_op jit(solution)/shard_map/while/body/eval_jaxpr/dot_general | solution.py:63
  95.4 48.2 %all-gather.6.cloned.1.call-done = bf16[2,768,768]{2,1,0:T(8,128)(2,1)} async-done(((bf16[2,192,768]{2,1,0:T(8,128)(2,1)}), bf16[2,768,768]{2,1,0:T(8,128)(2,1)}) %all-gather.6.cloned.1.call-update) | async-done | bytes 2359312 | tf_op jit(solution)/shard_map/all_gather | solution.py:189
  143.6 1.8 fusion.27
  145.3 1.6 fusion.26
  147.0 1.1 fusion.6
  148.1 1.1 fusion.5
  149.3 1.1 fusion.9
  150.3 1.1 fusion.8
  151.4 2.9 %copy.79 = f32[128,3840]{0,1:T(8,128)} copy(f32[128,3840]{1,0:T(8,128)} %fusion.8) | data formatting | bytes 3932160 | tf_op jit(solution)/shard_map/while/body/eval_jaxpr/concatenate | solution.py:115
  154.3 2.8 %copy.80 = f32[128,30,128]{2,0,1:T(8,128)} copy(f32[128,30,128]{0,2,1:T(8,128)} %bitcast.97) | data formatting | bytes 3932160 | tf_op jit(solution)/shard_map/while/body/eval_jaxpr/reshape | solution.py:230
  157.1 1.7 broadcast_multiply_fusion
  159.0 1.3 copy-done.2
  161.1 1.2 fusion
  162.3 2.2 %copy.81 = bf16[128,30,128]{0,2,1:T(8,128)(2,1)} copy(bf16[128,30,128]{2,0,1:T(8,128)(2,1)} %fusion) | data formatting | bytes 1966080 | tf_op jit(solution)/shard_map/while/body/eval_jaxpr/convert_element_type | solution.py:265
  164.5 3.2 %fusion.7 = bf16[128,3712]{1,0:T(8,128)(2,1)} fusion(bf16[896,1024]{1,0:T(8,128)(2,1)} %all-gather.4.cloned.1.call-done, bf16[128,3840]{0,1:T(8,128)(2,1)} %bitcast.110), kind=kOutput, calls=%fused_computation.23 | convolution fusion | flops 234995712 | bytes 2326528 | tf_op jit(solution)/shard_map/while/body/eval_jaxpr/dot_general | solution.py:67
  167.7 1.8 fusion.25
  170.8 1.2 fusion.12
  172.1 1.2 fusion.14
  173.3 1.1 fusion.16
  174.4 1.1 fusion.18
  175.5 2.1 copy.82
  177.6 1.9 copy.84
  179.5 2.5 %convolution_convert_fusion.3 = bf16[128,49,128]{2,1,0:T(8,128)(2,1)S(1)} fusion(bf16[128,29,49]{2,1,0:T(8,128)(2,1)S(1)} %copy.83, bf16[128,29,128]{2,1,0:T(8,128)(2,1)} %copy.84), kind=kOutput, calls=%fused_computation.8 | convolution fusion | flops 47366144 | bytes 2919680 | tf_op jit(solution)/shard_map/while/body/eval_jaxpr/erk,erc->ekc/dot_general | solution.py:273
  182.0 2.6 %copy.85 = bf16[128,49,128]{0,2,1:T(8,128)(2,1)} copy(bf16[128,49,128]{2,1,0:T(8,128)(2,1)S(1)} %convolution_convert_fusion.3) | data formatting | bytes 3211264 | tf_op jit(solution)/shard_map/while/body/eval_jaxpr/convert_element_type | solution.py:275
  184.7 1.9 fusion.2
  186.6 0.7 copy.86
  187.3 18.1 %reduce-scatter.4.cloned.1.call-done = f32[1,49,128]{2,1,0:T(8,128)} async-done(((f32[4,49,128]{2,1,0:T(8,128)}), f32[1,49,128]{2,1,0:T(8,128)}) %reduce-scatter.4.cloned.1.call-update) | async-done | bytes 25104
  205.5 1.4 add_convert_fusion
  (64 shorter events, 5.2 us)
Async XLA Ops:
  6.5 7.5 %copy-start = (bf16[128,512]{1,0:T(8,128)(2,1)S(1)}, bf16[128,512]{1,0:T(8,128)(2,1)}, u32[]{:S(2)}) copy-start(bf16[128,512]{1,0:T(8,128)(2,1)} %param.19) | copy-start | bytes 393220
  6.5 5.0 %copy-start.17 = (s32[1,1,128]{2,1,0:T(1,128)S(1)}, s32[1,1,128]{2,1,0:T(1,128)}, u32[]{:S(2)}) copy-start(s32[1,1,128]{2,1,0:T(1,128)} %param.27) | copy-start | bytes 1540
  6.5 58.0 %all-gather.8.cloned.1.call-start = ((), (), s32[]{:S(2)}) async-start(), calls=%async_computation.3 | async-start | bytes 2048000 | tf_op jit(solution)/shard_map/all_gather | solution.py:190
  7.3 85.3 %all-gather.4.cloned.1.call-start = ((), (), s32[]{:S(2)}) async-start(), calls=%async_computation.1 | async-start | bytes 2293760 | tf_op jit(solution)/shard_map/all_gather | solution.py:188
  8.0 135.6 %all-gather.6.cloned.1.call-start = ((), (), s32[]{:S(2)}) async-start(), calls=%async_computation.2 | async-start | bytes 2949120 | tf_op jit(solution)/shard_map/all_gather | solution.py:189
  8.7 196.7 %reduce-scatter.4.cloned.1.call-start = ((), (), s32[]{:S(2)}) async-start(), calls=%async_computation.4 | async-start | bytes 143360
  10.8 3.0 %copy-start.9 = (bf16[1,49,128]{2,1,0:T(8,128)(2,1)S(1)}, bf16[1,49,128]{2,1,0:T(8,128)(2,1)}, u32[]{:S(2)}) copy-start(bf16[1,49,128]{2,1,0:T(8,128)(2,1)} %param.18) | copy-start | bytes 37636
  10.8 3.0 %copy-start.11 = (bf16[49,196]{1,0:T(8,128)(2,1)S(1)}, bf16[49,196]{1,0:T(8,128)(2,1)}, u32[]{:S(2)}) copy-start(bf16[49,196]{1,0:T(8,128)(2,1)} %constant.36) | copy-start | bytes 57628
  10.8 3.2 %copy-start.8 = (bf16[196,49]{1,0:T(8,128)(2,1)S(1)}, bf16[196,49]{1,0:T(8,128)(2,1)}, u32[]{:S(2)}) copy-start(bf16[196,49]{1,0:T(8,128)(2,1)} %constant.37) | copy-start | bytes 57628
  10.8 3.2 %copy-start.12 = (bf16[1,49,128]{2,1,0:T(8,128)(2,1)S(1)}, bf16[1,49,128]{2,1,0:T(8,128)(2,1)}, u32[]{:S(2)}) copy-start(bf16[1,49,128]{2,1,0:T(8,128)(2,1)} %param.17) | copy-start | bytes 37636
  11.6 2.8 %copy-start.19 = (bf16[512,128]{1,0:T(8,128)(2,1)S(1)}, bf16[512,128]{1,0:T(8,128)(2,1)}, u32[]{:S(2)}) copy-start(bf16[512,128]{1,0:T(8,128)(2,1)} %param.20) | copy-start | bytes 393220
  13.8 11.9 %copy-start.16 = (s32[1,1,128]{2,1,0:T(1,128)S(1)}, s32[1,1,128]{2,1,0:T(1,128)}, u32[]{:S(2)}) copy-start(s32[1,1,128]{2,1,0:T(1,128)} %param.26) | copy-start | bytes 1540
  28.5 2.9 %copy-start.13 = (bf16[1,49,128]{2,1,0:T(8,128)(2,1)S(1)}, bf16[1,49,128]{2,1,0:T(8,128)(2,1)}, u32[]{:S(2)}) copy-start(bf16[1,49,128]{2,1,0:T(8,128)(2,1)} %param.16) | copy-start | bytes 37636
  28.5 16.9 %copy-start.14 = (s32[1,1,128]{2,1,0:T(1,128)S(1)}, s32[1,1,128]{2,1,0:T(1,128)}, u32[]{:S(2)}) copy-start(s32[1,1,128]{2,1,0:T(1,128)} %param.25) | copy-start | bytes 1540
  57.5 3.9 %copy-start.10 = (bf16[1,1,128,128]{3,2,1,0:T(8,128)(2,1)S(1)}, bf16[1,1,128,128]{3,2,1,0:T(8,128)(2,1)}, u32[]{:S(2)}) copy-start(bf16[1,1,128,128]{3,2,1,0:T(8,128)(2,1)} %param.28) | copy-start | bytes 98308
  62.0 2.5 %copy-start.5 = (bf16[128,29,128]{0,2,1:T(8,128)(2,1)S(1)}, bf16[128,29,128]{0,2,1:T(8,128)(2,1)}, u32[]{:S(2)}) copy-start(bf16[128,29,128]{0,2,1:T(8,128)(2,1)} %copy.78) | copy-start | bytes 2850820
  143.6 3.4 %copy-start.3 = (bf16[2,768,768]{2,1,0:T(8,128)(2,1)S(1)}, bf16[2,768,768]{2,1,0:T(8,128)(2,1)}, u32[]{:S(2)}) copy-start(bf16[2,768,768]{2,1,0:T(8,128)(2,1)} %all-gather.6.cloned.1.call-done) | copy-start | bytes 7077892
  143.6 3.4 %copy-start.6 = (bf16[128,29,128]{0,2,1:T(8,128)(2,1)S(1)}, bf16[128,29,128]{0,2,1:T(8,128)(2,1)}, u32[]{:S(2)}) copy-start(bf16[128,29,128]{0,2,1:T(8,128)(2,1)} %copy.78) | copy-start | bytes 2850820
  147.0 2.3 %copy-start.1 = (bf16[2,640,640]{2,1,0:T(8,128)(2,1)S(1)}, bf16[2,640,640]{2,1,0:T(8,128)(2,1)}, u32[]{:S(2)}) copy-start(bf16[2,640,640]{2,1,0:T(8,128)(2,1)} %all-gather.8.cloned.1.call-done) | copy-start | bytes 4915204
  158.8 1.5 copy-start.2
  164.5 3.2 %copy-start.7 = (bf16[128,30,128]{0,2,1:T(8,128)(2,1)S(1)}, bf16[128,30,128]{0,2,1:T(8,128)(2,1)}, u32[]{:S(2)}) copy-start(bf16[128,30,128]{0,2,1:T(8,128)(2,1)} %copy.81) | copy-start | bytes 2949124
  164.5 5.0 %copy-start.4 = (bf16[2,768,768]{2,1,0:T(8,128)(2,1)S(1)}, bf16[2,768,768]{2,1,0:T(8,128)(2,1)}, u32[]{:S(2)}) copy-start(bf16[2,768,768]{2,1,0:T(8,128)(2,1)} %all-gather.6.cloned.1.call-done) | copy-start | bytes 7077892
  182.0 2.6 %copy-start.15 = (s32[1,1,128]{2,1,0:T(1,128)S(1)}, s32[1,1,128]{2,1,0:T(1,128)}, u32[]{:S(2)}) copy-start(s32[1,1,128]{2,1,0:T(1,128)} %param.25) | copy-start | bytes 1540
  182.0 2.6 %copy-start.18 = (pred[128]{0:T(512)(128)(4,1)S(1)}, pred[128]{0:T(512)(128)(4,1)}, u32[]{:S(2)}) copy-start(pred[128]{0:T(512)(128)(4,1)} %iota_compare_fusion.6) | copy-start | bytes 388
Sparse Core Ops, SparseCore 0:
  8.9 41.7 all-gather.7
  52.3 40.2 all-gather.3
  94.2 49.3 all-gather.5
  187.4 17.9 reduce-scatter.3
where the time goes:
time: 214 us; the launch traced here: 213 us
  waiting for transfers between devices  93.5 us (44%)
  matrix products  36.7 us (17%)
  local copies, waits for them, and re-layouts  36.4 us (17%)
  blocking collectives  24.7 us (12%)
  between operations  14.2 us (7%)
  other arithmetic  7.85 us (4%)
    all_gather x1, waiting for transfers between devices, on_device(): lax.all_gather(so2_one, 'tgt', axis=1, tiled=True)  48.2 us
    all_gather x1, waiting for transfers between devices, on_device(): lax.all_gather(so2_zero, 'tgt', axis=0, tiled=True)  25.1 us
    unnamed x5, waiting for transfers between devices  20.2 us
    dot_general x13, matrix products, matmul_plain(): return jnp.dot(left, right, preferred_element_type=jnp.float32)  16.6 us
    all_gather x1, blocking collectives, on_device(): source_all = lax.all_gather(feat_in, 'tgt', axis=0, tiled=True)  14 us
    dot_general x10, matrix products, matmul_flip(): lax.dot_general(left, right, (((1,), (1,)), ((), ())), preferred_element_...  11.4 us
    all_gather x1, blocking collectives, on_device(): target_all = lax.all_gather(target_grad, 'src', axis=0, tiled=True)  10.7 us
  transfers between devices with their start and end apart: 4, of which 3 were waited for; matrix products, arithmetic and copies ran while one was open for 17% of the time, Pallas kernels for 0%

commit v1 on v0

--- a/solution.py
+++ b/solution.py
@@ -1,9 +1,12 @@
+import functools
 import math
 
 import jax
 import jax.numpy as jnp
 import numpy as np
 from jax import lax
+from jax.experimental import pallas as pl
+from jax.experimental.pallas import tpu as pltpu
 from jax.sharding import PartitionSpec as P
 
 LMAX = 6
@@ -296,6 +299,450 @@
     return (target_grad.astype(jnp.float32) + summed).astype(jnp.bfloat16)
 
 
+MESH = pl.DeviceIdType.MESH
+PAD = 64
+
+
+def plan_fits(n_src, so2_zero, so2_one, so2_two):
+    return (
+        n_src == 2**3
+        and so2_zero.shape[0] % 16 == 0
+        and so2_zero.shape[1] % 512 == 0
+        and so2_one.shape[1] % 32 == 0
+        and so2_two.shape[1] % 32 == 0
+    )
+
+
+def mm(left, right):
+    return jnp.dot(left, right, preferred_element_type=jnp.float32)
+
+
+def mm_nt(left, right):
+    return lax.dot_general(left, right, (((1,), (1,)), ((), ())), preferred_element_type=jnp.float32)
+
+
+def sigmoid(value):
+    return 1.0 / (1.0 + jnp.exp(-value))
+
+
+def fused_kernel(
+    n_src,
+    n_tgt,
+    to_grid,
+    from_grid_t,
+    to_grid_t,
+    feat,
+    ffn,
+    gout,
+    up,
+    down,
+    w0_in,
+    w1_in,
+    w2_in,
+    wig,
+    esrc,
+    etgt,
+    eang,
+    radial,
+    count,
+    out,
+    w0,
+    w1,
+    w2,
+    feat_all,
+    targ_all,
+    part,
+    recv_part,
+    xs_t,
+    z0,
+    z1,
+    z2,
+    grad_o,
+    hid,
+    g0,
+    g1,
+    g2,
+    wsend,
+    wrecv,
+    local_sem,
+    fsend,
+    frecv,
+    tsend,
+    trecv,
+    psend,
+    precv,
+):
+    i = lax.axis_index("src")
+    j = lax.axis_index("tgt")
+    y, x, core = i // 4, (i // 2) % 2, i % 2
+    bf, f32 = jnp.bfloat16, jnp.float32
+    coef, channels = feat.shape
+    slots = radial.shape[0]
+    angles = wig.shape[1]
+    kept = wig.shape[0]
+    rows0, rows1, rows2 = w0_in.shape[0], w1_in.shape[1], w2_in.shape[1]
+    cols0 = w0_in.shape[1] // 4
+
+    def chip_index(yy, xx, cc):
+        return yy * 4 + xx * 2 + cc
+
+    to_x = (chip_index(y, 1 - x, core), j)
+    to_y = (chip_index(1 - y, x, core), j)
+    to_core = (chip_index(y, x, 1 - core), j)
+    z_peers = [(i, (j + t) % n_tgt) for t in range(1, n_tgt)]
+    plane_peers = [((i + t) % n_src, j) for t in range(1, n_src)]
+
+    barrier = pltpu.get_barrier_semaphore()
+    for peer in z_peers + plane_peers:
+        pl.semaphore_signal(barrier, inc=1, device_id=peer, device_id_type=MESH)
+
+    locals_ = [
+        pltpu.make_async_copy(w0_in, w0.at[pl.ds(pl.multiple_of(j * rows0, 16), rows0), :], local_sem.at[0]),
+        pltpu.make_async_copy(w1_in, w1.at[:, pl.ds(pl.multiple_of(j * rows1, 16), rows1), :], local_sem.at[1]),
+        pltpu.make_async_copy(w2_in, w2.at[:, pl.ds(pl.multiple_of(j * rows2, 16), rows2), :], local_sem.at[2]),
+    ]
+    for copy in locals_:
+        copy.start()
+
+    spread = (
+        lax.broadcasted_iota(jnp.int32, (PAD, coef), 0) == lax.broadcasted_iota(jnp.int32, (PAD, coef), 1)
+    ).astype(bf)
+    feat_all[pl.ds(pl.multiple_of(j * PAD, PAD), PAD), :] = mm(spread, feat[...]).astype(bf)
+
+    pl.semaphore_wait(barrier, len(z_peers) + len(plane_peers))
+
+    def remote(source, target, send, recv, peer):
+        return pltpu.make_async_remote_copy(
+            src_ref=source, dst_ref=target, send_sem=send, recv_sem=recv, device_id=peer, device_id_type=MESH
+        )
+
+    def piece(c, shard, yy, xx):
+        if c == 0:
+            half = rows1 // 2
+            return [w1.at[yy, pl.ds(pl.multiple_of(shard * rows1 + xx * half, 16), half), :]]
+        half = rows2 // 2
+        return [
+            w0.at[
+                pl.ds(pl.multiple_of(shard * rows0, 16), rows0),
+                pl.ds(pl.multiple_of((yy * 2 + xx) * cols0, 128), cols0),
+            ],
+            w2.at[yy, pl.ds(pl.multiple_of(shard * rows2 + xx * half, 16), half), :],
+        ]
+
+    def own_piece(c):
+        if c == 0:
+            half = rows1 // 2
+            return [w1_in.at[y, pl.ds(pl.multiple_of(x * half, 16), half), :]]
+        half = rows2 // 2
+        return [
+            w0_in.at[:, pl.ds(pl.multiple_of((y * 2 + x) * cols0, 128), cols0)],
+            w2_in.at[y, pl.ds(pl.multiple_of(x * half, 16), half), :],
+        ]
+
+    def origin(o):
+        return (1 - y if o >= 2 else y, 1 - x if o % 2 else x)
+
+    def piece_from(c, t, o):
+        yy, xx = origin(o)
+        return piece(c, (j + n_tgt - t) % n_tgt, yy, xx)
+
+    def start_z(c):
+        for t in range(1, n_tgt):
+            for a, (source, target) in enumerate(zip(own_piece(c), piece(c, j, y, x))):
+                remote(source, target, wsend.at[t - 1, 0, a], wrecv.at[0, t - 1, 0, a], z_peers[t - 1]).start()
+
+    def send(c, t, o, slot, kind, to_o, peer):
+        for a, ref in enumerate(piece_from(c, t, o)):
+            remote(ref, ref, wsend.at[t - 1, slot, a], wrecv.at[kind, t - 1, to_o, a], peer).start()
+
+    def arrive(c, t, o, kind):
+        for a, ref in enumerate(piece_from(c, t, o)):
+            remote(ref, ref, wsend.at[t - 1, 0, a], wrecv.at[kind, t - 1, o, a], to_core).wait_recv()
+
+    def relay_own(c, t):
+        arrive(c, t, 0, 0)
+        send(c, t, 0, 1, 0, 1, to_x)
+        send(c, t, 0, 2, 0, 2, to_y)
+        send(c, t, 0, 4, 1, 0, to_core)
+
+    def relay(c, t):
+        arrive(c, t, 1, 0)
+        if c == 0:
+            send(c, t, 1, 3, 0, 3, to_y)
+        send(c, t, 1, 5, 1, 1, to_core)
+        arrive(c, t, 2, 0)
+        if c == 1:
+            send(c, t, 2, 3, 0, 3, to_x)
+        send(c, t, 2, 6, 1, 2, to_core)
+
+    def relay_diag(c, t):
+        arrive(c, t, 3, 0)
+        send(c, t, 3, 7, 1, 3, to_core)
+
+    def finish(c):
+        for t in order:
+            for o in range(4):
+                arrive(1 - c, t, o, 1)
+
+    def drain(c):
+        for t in range(1, n_tgt):
+            for slot in range(8):
+                for a, ref in enumerate(piece_from(c, t, 0)):
+                    remote(ref, ref, wsend.at[t - 1, slot, a], wrecv.at[0, t - 1, 0, a], to_core).wait_send()
+
+    def by_core(function, *args):
+        for c in range(2):
+            pl.when(core == c)(functools.partial(function, c, *args))
+
+    order = [1, n_tgt - 1] + list(range(2, n_tgt - 1))
+    feat_own = feat_all.at[pl.ds(pl.multiple_of(j * PAD, PAD), PAD), :]
+    feat_sends = [
+        remote(feat_own, feat_own, fsend.at[t - 1], frecv.at[t - 1], z_peers[t - 1]) for t in range(1, n_tgt)
+    ]
+    for copy in feat_sends:
+        copy.start()
+    by_core(start_z)
+
+    grid_in = mm(to_grid[...], ffn[...]).astype(bf)
+    pre = mm(grid_in, up[...])
+    value = mm(from_grid_t[...], gout[...]).astype(bf)
+    grad_act = mm_nt(value, down[...])
+    sig = sigmoid(pre)
+    grad_pre = (grad_act * sig * (1.0 + pre * (1.0 - sig))).astype(bf)
+    grad_grid = mm_nt(grad_pre, up[...]).astype(bf)
+    target = (mm(spread, gout[...]) + mm(to_grid_t[...], grad_grid)).astype(bf)
+    targ_all[pl.ds(pl.multiple_of(i * PAD, PAD), PAD), :] = target
+    targ_own = targ_all.at[pl.ds(pl.multiple_of(i * PAD, PAD), PAD), :]
+    targ_sends = [
+        remote(targ_own, targ_own, tsend.at[t - 1], trecv.at[t - 1], plane_peers[t - 1]) for t in range(1, n_src)
+    ]
+    for copy in targ_sends:
+        copy.start()
+
+    by_core(relay_own, order[0])
+
+    def iota(shape, axis):
+        return lax.broadcasted_iota(jnp.int32, shape, axis)
+
+    eye = (iota((slots, slots), 0) == iota((slots, slots), 1)).astype(bf)
+    pick_angle_t = (iota((angles, slots), 0) == eang[...]).astype(bf)
+    n_s, n_t = n_tgt * PAD, n_src * PAD
+    live = iota((1, slots), 1) < count[...]
+    mask_s_t = ((iota((n_s, slots), 0) // PAD == esrc[...]) & live).astype(bf)
+    mask_t_t = (iota((n_t, slots), 0) // PAD == etgt[...]).astype(bf)
+    pick_angle = mm_nt(eye, pick_angle_t).astype(bf)
+    mask_s = mm_nt(eye, mask_s_t).astype(bf)
+    mask_t = mm_nt(eye, mask_t_t).astype(bf)
+    spread_s = (iota((coef, n_s), 1) % PAD == iota((coef, n_s), 0)).astype(bf)
+    spread_t = (iota((coef, n_t), 1) % PAD == iota((coef, n_t), 0)).astype(bf)
+    spread_s_t = (iota((n_s, coef), 0) % PAD == iota((n_s, coef), 1)).astype(bf)
+
+    by_core(relay_own, order[1])
+    for r in range(kept):
+        wide = mm_nt(spread_s_t, wig[r]).astype(bf)
+        xs_t[:, r * slots : (r + 1) * slots] = mm(wide, pick_angle_t).astype(bf) * mask_s_t
+    for t in range(2, n_tgt - 1):
+        by_core(relay_own, t)
+
+    for copy in feat_sends:
+        copy.wait_recv()
+    feats = feat_all[...]
+    degree_cut = [7, 13, 19, 24, 29]
+    for r in range(kept):
+        turn = mm(mm(pick_angle, wig[r]).astype(bf), spread_s).astype(bf) * mask_s
+        row = mm(turn, feats).astype(bf)
+        if r < degree_cut[0]:
+            z0[:, r * channels : (r + 1) * channels] = row
+        elif r < degree_cut[2]:
+            p, at = divmod(r - degree_cut[0], 6)
+            z1[p * slots : (p + 1) * slots, at * channels : (at + 1) * channels] = row
+        else:
+            p, at = divmod(r - degree_cut[2], 5)
+            z2[p * slots : (p + 1) * slots, at * channels : (at + 1) * channels] = row
+    by_core(relay, order[0])
+
+    for copy in targ_sends:
+        copy.wait_recv()
+    targets = targ_all[...]
+    for r in range(kept):
+        turn = mm(mm(pick_angle, wig[r]).astype(bf), spread_t).astype(bf) * mask_t
+        grad_o[r] = mm(turn, targets) * message_scale
+        if r == 9:
+            by_core(relay, order[1])
+        if r == 19:
+            by_core(relay_diag, order[0])
+    for t in range(2, n_tgt - 1):
+        by_core(relay, t)
+    by_core(relay_diag, order[1])
+    for t in range(2, n_tgt - 1):
+        by_core(relay_diag, t)
+    for copy in locals_:
+        copy.wait()
+    by_core(finish)
+
+    gain = radial[...].astype(f32)
+    h0 = mm(z0[...], w0[...])
+    for r in range(8):
+        hid[r] = h0[:, r * channels : (r + 1) * channels] * gain
+    for first, per, zz, ww in ((8, 6, z1, w1), (20, 5, z2, w2)):
+        real = mm(zz[...], ww[0])
+        imag = mm(zz[...], ww[1])
+        plus = real[:slots] - imag[slots:]
+        minus = real[slots:] + imag[:slots]
+        for r in range(per):
+            cut = slice(r * channels, (r + 1) * channels)
+            hid[first + r] = plus[:, cut] * gain
+            hid[first + per + r] = minus[:, cut] * gain
+
+    sig_gate = sigmoid(hid[7])
+    scalar = hid[0]
+    sig_scalar = sigmoid(scalar)
+    g0[:, :channels] = (grad_o[0] * sig_scalar * (1.0 + scalar * (1.0 - sig_scalar)) * gain).astype(bf)
+    gate_gain = sig_gate * gain
+    total = jnp.zeros((slots, channels), f32)
+    for r in range(1, kept):
+        row = grad_o[r]
+        total = total + row * hid[r if r < 7 else r + 1]
+        value_r = (row * gate_gain).astype(bf)
+        if r < 7:
+            g0[:, r * channels : (r + 1) * channels] = value_r
+        elif r < 19:
+            p, at = divmod(r - 7, 6)
+            g1[p * slots : (p + 1) * slots, at * channels : (at + 1) * channels] = value_r
+        else:
+            p, at = divmod(r - 19, 5)
+            g2[p * slots : (p + 1) * slots, at * channels : (at + 1) * channels] = value_r
+    g0[:, 7 * channels :] = (total * sig_gate * (1.0 - sig_gate) * gain).astype(bf)
+
+    back = mm_nt(g0[...], w0[...]).astype(bf)
+    rows = [back[:, r * channels : (r + 1) * channels] for r in range(7)]
+    for per, gg, ww in ((6, g1, w1), (5, g2, w2)):
+        real = mm_nt(gg[...], ww[0])
+        imag = mm_nt(gg[...], ww[1])
+        plus = (real[:slots] + imag[slots:]).astype(bf)
+        minus = (real[slots:] - imag[:slots]).astype(bf)
+        rows += [plus[:, r * channels : (r + 1) * channels] for r in range(per)]
+        rows += [minus[:, r * channels : (r + 1) * channels] for r in range(per)]
+    part[...] = mm(xs_t[...], jnp.concatenate(rows, axis=0))
+
+    part_sends = [
+        remote(
+            part.at[pl.ds(pl.multiple_of(((j + t) % n_tgt) * PAD, PAD), PAD), :],
+            recv_part.at[t - 1],
+            psend.at[t - 1],
+            precv.at[t - 1],
+            z_peers[t - 1],
+        )
+        for t in range(1, n_tgt)
+    ]
+    for copy in part_sends:
+        copy.start()
+    by_core(drain)
+    for copy in feat_sends + targ_sends:
+        copy.wait_send()
+    summed = part[pl.ds(pl.multiple_of(j * PAD, PAD), PAD), :]
+    for t, copy in enumerate(part_sends):
+        copy.wait_recv()
+        summed = summed + recv_part[t]
+    mine = targ_all[pl.ds(pl.multiple_of(i * PAD, PAD), PAD), :].astype(f32)
+    out[...] = (mine + summed)[:coef].astype(bf)
+    for copy in part_sends:
+        copy.wait_send()
+
+
+def fused_on_device(
+    feat_in,
+    ffn_in,
+    grad_out,
+    ffn_up,
+    ffn_down,
+    so2_zero,
+    so2_one,
+    so2_two,
+    wigner,
+    edge_src,
+    edge_tgt,
+    edge_angle,
+    edge_radial,
+    edge_count,
+):
+    n_src, n_tgt = lax.axis_size("src"), lax.axis_size("tgt")
+    _, coef, channels = feat_in.shape
+    kept = wigner.shape[1]
+    slots = edge_src.shape[2]
+    to_grid, from_grid = sphere_tables(LMAX, GRID_SIDE)
+    more = -to_grid.shape[0] % 16
+    to_grid = jnp.pad(to_grid, ((0, more), (0, 0)))
+    from_grid_t = jnp.pad(from_grid.T, ((0, more), (0, 0)))
+    to_grid_t = jnp.pad(to_grid.T, ((0, PAD - coef), (0, 0)))
+    bf, f32 = jnp.bfloat16, jnp.float32
+    k0, k1, k2 = so2_zero.shape[0] * n_tgt, so2_one.shape[1] * n_tgt, so2_two.shape[1] * n_tgt
+    vmem = pl.BlockSpec(memory_space=pltpu.VMEM)
+    hbm = pl.BlockSpec(memory_space=pl.ANY)
+    dma = pltpu.SemaphoreType.DMA
+    result = pl.pallas_call(
+        functools.partial(fused_kernel, n_src, n_tgt),
+        out_shape=jax.ShapeDtypeStruct((coef, channels), bf),
+        in_specs=[vmem] * 8 + [hbm] * 3 + [vmem] * 6,
+        out_specs=vmem,
+        scratch_shapes=[
+            pltpu.VMEM((k0, so2_zero.shape[1]), bf),
+            pltpu.VMEM((2, k1, so2_one.shape[2]), bf),
+            pltpu.VMEM((2, k2, so2_two.shape[2]), bf),
+            pltpu.VMEM((n_tgt * PAD, channels), bf),
+            pltpu.VMEM((n_src * PAD, channels), bf),
+            pltpu.VMEM((n_tgt * PAD, channels), f32),
+            pltpu.VMEM((n_tgt - 1, PAD, channels), f32),
+            pltpu.VMEM((n_tgt * PAD, kept * slots), bf),
+            pltpu.VMEM((slots, k0), bf),
+            pltpu.VMEM((2 * slots, k1), bf),
+            pltpu.VMEM((2 * slots, k2), bf),
+            pltpu.VMEM((kept, slots, channels), f32),
+            pltpu.VMEM((kept + 1, slots, channels), f32),
+            pltpu.VMEM((slots, so2_zero.shape[1]), bf),
+            pltpu.VMEM((2 * slots, k1), bf),
+            pltpu.VMEM((2 * slots, k2), bf),
+            dma((n_tgt - 1, 8, 2)),
+            dma((2, n_tgt - 1, 4, 2)),
+            dma((3,)),
+            dma((n_tgt - 1,)),
+            dma((n_tgt - 1,)),
+            dma((n_src - 1,)),
+            dma((n_src - 1,)),
+            dma((n_tgt - 1,)),
+            dma((n_tgt - 1,)),
+        ],
+        compiler_params=pltpu.CompilerParams(
+            collective_id=0, has_side_effects=True, vmem_limit_bytes=48 * 1024 * 1024
+        ),
+    )(
+        to_grid,
+        from_grid_t,
+        to_grid_t,
+        feat_in.reshape(coef, channels),
+        ffn_in.reshape(coef, channels),
+        grad_out.reshape(coef, channels),
+        ffn_up,
+        ffn_down,
+        so2_zero,
+        so2_one,
+        so2_two,
+        wigner.transpose(1, 0, 2),
+        edge_src.reshape(1, slots),
+        edge_tgt.reshape(1, slots),
+        edge_angle.reshape(1, slots),
+        edge_radial.reshape(slots, channels),
+        edge_count,
+    )
+    return result.reshape(feat_in.shape)
+
+
+def choose(*args):
+    if plan_fits(lax.axis_size("src"), *args[5:8]):
+        return fused_on_device(*args)
+    return on_device(*args)
+
+
 def solution(mesh):
     placed = (
         P(("src", "tgt"), None, None),
@@ -314,7 +761,7 @@
         P("src", "tgt"),
     )
     return jax.shard_map(
-        on_device,
+        choose,
         mesh=mesh,
         in_specs=placed,
         out_specs=P(("src", "tgt"), None, None),

time: 214 us -> 62.6 us (0.29)
  waiting for transfers between devices: 93.5 us -> 0 us
  Pallas kernels: 0 us -> 52 us
  matrix products: 36.7 us -> 0 us
  local copies, waits for them, and re-layouts: 36.4 us -> 9.29 us
  blocking collectives: 24.7 us -> 0 us
  between operations: 14.2 us -> 0.81 us
  other arithmetic: 7.85 us -> 0 us
    all_gather x3 -> x0, waiting for transfers between devices: 73.2 us -> none  [the longest x1 48.2 us: on_device(): lax.all_gather(so2_one, 'tgt', axis=1, tiled=True)]
    pallas_call x0 -> x1, Pallas kernels: none -> 52 us  [fused_on_device(): pl.pallas_call(functools.partial(fused_kernel, n_src, n_tgt), out_shape=j...]
    dot_general x29 -> x0, matrix products: 36.7 us -> none  [the longest x13 16.6 us: matmul_plain(): return jnp.dot(left, right, preferred_element_type=jnp.float32)]
    all_gather x2 -> x0, blocking collectives: 24.7 us -> none  [the longest x1 14 us: on_device(): source_all = lax.all_gather(feat_in, 'tgt', axis=0, tiled=True)]
    unnamed x5 -> x0, waiting for transfers between devices: 20.2 us -> none
    convert_element_type x6 -> x0, local copies, waits for them, and re-layouts: 15.4 us -> none  [the longest x1 3.67 us: rotate_block(): source_rows = matmul_plain(pick_source, source_flat).astype(jnp.bfloat16)...]
    reshape x6 -> x0, local copies, waits for them, and re-layouts: 11.7 us -> none  [the longest x1 3.47 us: rotate_block(): source_rows = matmul_plain(pick_source, source_flat).astype(jnp.bfloat16)...]
    unnamed x41 -> x32, local copies, waits for them, and re-layouts: 3.4 us -> 9.29 us
  transfers between devices with their start and end apart: 4 -> 0, of which waited for: 3 -> 0; matrix products, arithmetic and copies ran while one was open for 17% -> 0% of each run, Pallas kernels for 0% -> 0%
where the time goes in v1:
time: 62.6 us; the launch traced here: 62.1 us
  Pallas kernels  52 us (83%)
  local copies, waits for them, and re-layouts  9.29 us (15%)
  between operations  0.81 us (1%)
    pallas_call x1, Pallas kernels, fused_on_device(): pl.pallas_call(functools.partial(fused_kernel, n_src, n_tgt), out_shape=j...  52 us
    unnamed x32, local copies, waits for them, and re-layouts  9.29 us

profile of v1, /device:TPU:0, one launch (start us, length us, event | category | flops | bytes accessed | tf_op | source)
XLA Modules:
  0.0 62.1 jit_solution(14726291665732926698)
XLA Ops:
  0.0 0.0 copy-start
  0.7 0.0 copy-start.3
  0.7 0.0 copy-start.4
  0.7 0.0 copy-start.7
  0.7 1.5 %copy.17 = bf16[64,29,49]{2,0,1:T(8,128)(2,1)S(1)} copy(bf16[64,29,49]{0,1,2:T(8,128)(2,1)} %param.24) | data formatting | bytes 363776 | tf_op args[8]
  2.3 0.0 copy-start.12
  2.3 0.0 copy-start.13
  2.3 0.0 copy-start.14
  2.3 0.0 copy-done
  2.3 0.0 copy-done.3
  2.3 0.0 copy-done.4
  2.3 0.0 copy-done.7
  2.3 0.6 copy-done.12
  2.9 0.0 copy-done.13
  2.9 0.0 copy-done.14
  3.0 0.0 copy-start.1
  3.0 1.0 %copy-done.1 = bf16[224,1024]{1,0:T(8,128)(2,1)S(1)} copy-done((bf16[224,1024]{1,0:T(8,128)(2,1)S(1)}, bf16[224,1024]{1,0:T(8,128)(2,1)}, u32[]{:S(2)}) %copy-start.1) | copy-done | bytes 458776
  4.0 0.0 copy-start.2
  4.0 1.0 %copy-done.2 = bf16[2,160,640]{2,1,0:T(8,128)(2,1)S(1)} copy-done((bf16[2,160,640]{2,1,0:T(8,128)(2,1)S(1)}, bf16[2,160,640]{2,1,0:T(8,128)(2,1)}, u32[]{:S(2)}) %copy-start.2) | copy-done | bytes 409624
  5.0 0.0 copy-start.5
  5.0 0.8 %copy-done.5 = bf16[208,49]{1,0:T(8,128)(2,1)S(1)} copy-done((bf16[208,49]{1,0:T(8,128)(2,1)S(1)}, bf16[208,49]{1,0:T(8,128)(2,1)}, u32[]{:S(2)}) %copy-start.5) | copy-done | bytes 20408
  5.8 0.0 copy-start.6
  5.8 0.8 %copy-done.6 = bf16[208,49]{1,0:T(8,128)(2,1)S(1)} copy-done((bf16[208,49]{1,0:T(8,128)(2,1)S(1)}, bf16[208,49]{1,0:T(8,128)(2,1)}, u32[]{:S(2)}) %copy-start.6) | copy-done | bytes 20408
  6.6 0.0 copy-start.8
  6.6 0.8 %copy-done.8 = bf16[64,208]{1,0:T(8,128)(2,1)S(1)} copy-done((bf16[64,208]{1,0:T(8,128)(2,1)S(1)}, bf16[64,208]{1,0:T(8,128)(2,1)}, u32[]{:S(2)}) %copy-start.8) | copy-done | bytes 26648
  7.4 0.0 copy-start.9
  7.4 0.7 %copy-done.9 = bf16[1,49,128]{2,1,0:T(8,128)(2,1)S(1)} copy-done((bf16[1,49,128]{2,1,0:T(8,128)(2,1)S(1)}, bf16[1,49,128]{2,1,0:T(8,128)(2,1)}, u32[]{:S(2)}) %copy-start.9) | copy-done | bytes 12568
  8.1 0.0 copy-start.10
  8.1 0.7 %copy-done.10 = bf16[1,49,128]{2,1,0:T(8,128)(2,1)S(1)} copy-done((bf16[1,49,128]{2,1,0:T(8,128)(2,1)S(1)}, bf16[1,49,128]{2,1,0:T(8,128)(2,1)}, u32[]{:S(2)}) %copy-start.10) | copy-done | bytes 12568
  8.8 0.0 copy-start.11
  8.8 0.7 %copy-done.11 = bf16[1,49,128]{2,1,0:T(8,128)(2,1)S(1)} copy-done((bf16[1,49,128]{2,1,0:T(8,128)(2,1)S(1)}, bf16[1,49,128]{2,1,0:T(8,128)(2,1)}, u32[]{:S(2)}) %copy-start.11) | copy-done | bytes 12568
  9.5 52.0 %shard_map.154 = bf16[49,128]{1,0:T(8,128)(2,1)S(1)} custom-call(bf16[208,49]{1,0:T(8,128)(2,1)S(1)} %copy-done.6, bf16[208,49]{1,0:T(8,128)(2,1)S(1)} %copy-done.5, bf16[64,208]{1,0:T(8,128)(2,1)S(1)} %copy-done.8, bf16[49,128]{1,0:T(8,128)(2,1)S(1)} %bitcast.12, bf16[49,128]{1,0:T(8,128)(2,1)S(1)} %bitcast.13, bf16[49,128]{1,0:T(8,128)(2,1)S(1)} %bitcast.14, ...), custom_call_target="tpu_custom_call" | custom-call | tf_op jit(solution)/shard_map/pallas_call | solution.py:683
  61.5 0.6 copy.20
Async XLA Ops:
  0.0 2.3 %copy-start = (bf16[2,192,768]{2,1,0:T(8,128)(2,1)S(1)}, bf16[2,192,768]{2,1,0:T(8,128)(2,1)}, u32[]{:S(2)}) copy-start(bf16[2,192,768]{2,1,0:T(8,128)(2,1)} %w1_in.1) | copy-start | bytes 1769476
  0.7 1.6 %copy-start.3 = (bf16[128,512]{1,0:T(8,128)(2,1)S(1)}, bf16[128,512]{1,0:T(8,128)(2,1)}, u32[]{:S(2)}) copy-start(bf16[128,512]{1,0:T(8,128)(2,1)} %up.1) | copy-start | bytes 393220
  0.7 1.6 %copy-start.4 = (bf16[512,128]{1,0:T(8,128)(2,1)S(1)}, bf16[512,128]{1,0:T(8,128)(2,1)}, u32[]{:S(2)}) copy-start(bf16[512,128]{1,0:T(8,128)(2,1)} %down.1) | copy-start | bytes 393220
  0.7 1.6 %copy-start.7 = (bf16[1,1,128,128]{3,2,1,0:T(8,128)(2,1)S(1)}, bf16[1,1,128,128]{3,2,1,0:T(8,128)(2,1)}, u32[]{:S(2)}) copy-start(bf16[1,1,128,128]{3,2,1,0:T(8,128)(2,1)} %param.28) | copy-start | bytes 98308
  2.3 0.7 %copy-start.12 = (s32[1,1,128]{2,1,0:T(1,128)S(1)}, s32[1,1,128]{2,1,0:T(1,128)}, u32[]{:S(2)}) copy-start(s32[1,1,128]{2,1,0:T(1,128)} %param.25) | copy-start | bytes 1540
  2.3 0.7 %copy-start.13 = (s32[1,1,128]{2,1,0:T(1,128)S(1)}, s32[1,1,128]{2,1,0:T(1,128)}, u32[]{:S(2)}) copy-start(s32[1,1,128]{2,1,0:T(1,128)} %param.26) | copy-start | bytes 1540
  2.3 0.7 %copy-start.14 = (s32[1,1,128]{2,1,0:T(1,128)S(1)}, s32[1,1,128]{2,1,0:T(1,128)}, u32[]{:S(2)}) copy-start(s32[1,1,128]{2,1,0:T(1,128)} %param.27) | copy-start | bytes 1540
  3.0 1.0 %copy-start.1 = (bf16[224,1024]{1,0:T(8,128)(2,1)S(1)}, bf16[224,1024]{1,0:T(8,128)(2,1)}, u32[]{:S(2)}) copy-start(bf16[224,1024]{1,0:T(8,128)(2,1)} %w0_in.1) | copy-start | bytes 1376260
  4.0 1.0 %copy-start.2 = (bf16[2,160,640]{2,1,0:T(8,128)(2,1)S(1)}, bf16[2,160,640]{2,1,0:T(8,128)(2,1)}, u32[]{:S(2)}) copy-start(bf16[2,160,640]{2,1,0:T(8,128)(2,1)} %w2_in.1) | copy-start | bytes 1228804
  5.0 0.8 %copy-start.5 = (bf16[208,49]{1,0:T(8,128)(2,1)S(1)}, bf16[208,49]{1,0:T(8,128)(2,1)}, u32[]{:S(2)}) copy-start(bf16[208,49]{1,0:T(8,128)(2,1)} %constant.27.from_grid_t) | copy-start | bytes 61156
  5.8 0.8 %copy-start.6 = (bf16[208,49]{1,0:T(8,128)(2,1)S(1)}, bf16[208,49]{1,0:T(8,128)(2,1)}, u32[]{:S(2)}) copy-start(bf16[208,49]{1,0:T(8,128)(2,1)} %constant.24.to_grid) | copy-start | bytes 61156
  6.6 0.8 %copy-start.8 = (bf16[64,208]{1,0:T(8,128)(2,1)S(1)}, bf16[64,208]{1,0:T(8,128)(2,1)}, u32[]{:S(2)}) copy-start(bf16[64,208]{1,0:T(8,128)(2,1)} %constant.29.to_grid_t) | copy-start | bytes 79876
  7.4 0.7 %copy-start.9 = (bf16[1,49,128]{2,1,0:T(8,128)(2,1)S(1)}, bf16[1,49,128]{2,1,0:T(8,128)(2,1)}, u32[]{:S(2)}) copy-start(bf16[1,49,128]{2,1,0:T(8,128)(2,1)} %param.16) | copy-start | bytes 37636
  8.1 0.7 %copy-start.10 = (bf16[1,49,128]{2,1,0:T(8,128)(2,1)S(1)}, bf16[1,49,128]{2,1,0:T(8,128)(2,1)}, u32[]{:S(2)}) copy-start(bf16[1,49,128]{2,1,0:T(8,128)(2,1)} %param.17) | copy-start | bytes 37636
  8.8 0.7 %copy-start.11 = (bf16[1,49,128]{2,1,0:T(8,128)(2,1)S(1)}, bf16[1,49,128]{2,1,0:T(8,128)(2,1)}, u32[]{:S(2)}) copy-start(bf16[1,49,128]{2,1,0:T(8,128)(2,1)} %param.18) | copy-start | bytes 37636

commit v2 on v1

--- a/solution.py
+++ b/solution.py
@@ -303,9 +303,10 @@
 PAD = 64
 
 
-def plan_fits(n_src, so2_zero, so2_one, so2_two):
+def plan_fits(n_src, n_tgt, so2_zero, so2_one, so2_two):
     return (
         n_src == 2**3
+        and n_tgt == 2**2
         and so2_zero.shape[0] % 16 == 0
         and so2_zero.shape[1] % 512 == 0
         and so2_one.shape[1] % 32 == 0
@@ -328,6 +329,24 @@
 def fused_kernel(
     n_src,
     n_tgt,
+    to_grid_in,
+    from_grid_t_in,
+    to_grid_t_in,
+    feat_in,
+    ffn_in,
+    gout_in,
+    up_in,
+    down_in,
+    w0_in,
+    w1_in,
+    w2_in,
+    wig_in,
+    esrc_in,
+    etgt_in,
+    eang_in,
+    radial_in,
+    count,
+    out,
     to_grid,
     from_grid_t,
     to_grid_t,
@@ -336,16 +355,12 @@
     gout,
     up,
     down,
-    w0_in,
-    w1_in,
-    w2_in,
     wig,
     esrc,
     etgt,
     eang,
     radial,
-    count,
-    out,
+    in_sem,
     w0,
     w1,
     w2,
@@ -353,6 +368,8 @@
     targ_all,
     part,
     recv_part,
+    table_s,
+    table_t,
     xs_t,
     z0,
     z1,
@@ -362,6 +379,7 @@
     g0,
     g1,
     g2,
+    osend,
     wsend,
     wrecv,
     local_sem,
@@ -392,6 +410,25 @@
     z_peers = [(i, (j + t) % n_tgt) for t in range(1, n_tgt)]
     plane_peers = [((i + t) % n_src, j) for t in range(1, n_src)]
 
+    staged = {}
+    for at, (name, source, target) in enumerate((
+        ("feat", feat_in, feat),
+        ("ffn", ffn_in, ffn),
+        ("gout", gout_in, gout),
+        ("to_grid", to_grid_in, to_grid),
+        ("from_grid_t", from_grid_t_in, from_grid_t),
+        ("up", up_in, up),
+        ("down", down_in, down),
+        ("to_grid_t", to_grid_t_in, to_grid_t),
+        ("esrc", esrc_in, esrc),
+        ("etgt", etgt_in, etgt),
+        ("eang", eang_in, eang),
+        ("wig", wig_in, wig),
+        ("radial", radial_in, radial),
+    )):
+        staged[name] = pltpu.make_async_copy(source, target, in_sem.at[at])
+        staged[name].start()
+
     barrier = pltpu.get_barrier_semaphore()
     for peer in z_peers + plane_peers:
         pl.semaphore_signal(barrier, inc=1, device_id=peer, device_id_type=MESH)
@@ -407,6 +444,7 @@
     spread = (
         lax.broadcasted_iota(jnp.int32, (PAD, coef), 0) == lax.broadcasted_iota(jnp.int32, (PAD, coef), 1)
     ).astype(bf)
+    staged["feat"].wait()
     feat_all[pl.ds(pl.multiple_of(j * PAD, PAD), PAD), :] = mm(spread, feat[...]).astype(bf)
 
     pl.semaphore_wait(barrier, len(z_peers) + len(plane_peers))
@@ -446,21 +484,54 @@
         yy, xx = origin(o)
         return piece(c, (j + n_tgt - t) % n_tgt, yy, xx)
 
+    last = n_tgt - 1
+    lowest, highest = (last - j) // last, j // last
+    t_first = 1 + 2 * lowest
+    t_third = 2 - lowest + highest
+    order = [t_first, 6 - t_first - t_third, t_third]
+    above, below = (i, (j + 1) % n_tgt), (i, (j + n_tgt - 1) % n_tgt)
+
+    def own_copies(c, up_way):
+        t, peer = (1, above) if up_way else (last, below)
+        return [
+            remote(source, target, osend.at[int(up_way), a], wrecv.at[0, t - 1, 0, a], peer)
+            for a, (source, target) in enumerate(zip(own_piece(c), piece(c, j, y, x)))
+        ]
+
     def start_z(c):
-        for t in range(1, n_tgt):
-            for a, (source, target) in enumerate(zip(own_piece(c), piece(c, j, y, x))):
-                remote(source, target, wsend.at[t - 1, 0, a], wrecv.at[0, t - 1, 0, a], z_peers[t - 1]).start()
+        @pl.when(j < last)
+        def _():
+            for copy in own_copies(c, True):
+                copy.start()
+
+        @pl.when(j > 0)
+        def _():
+            for copy in own_copies(c, False):
+                copy.start()
 
     def send(c, t, o, slot, kind, to_o, peer):
         for a, ref in enumerate(piece_from(c, t, o)):
             remote(ref, ref, wsend.at[t - 1, slot, a], wrecv.at[kind, t - 1, to_o, a], peer).start()
 
+    def onward(c, t, to_t, peer):
+        for a, ref in enumerate(piece_from(c, t, 0)):
+            remote(ref, ref, wsend.at[t - 1, 0, a], wrecv.at[0, to_t - 1, 0, a], peer).start()
+
     def arrive(c, t, o, kind):
         for a, ref in enumerate(piece_from(c, t, o)):
             remote(ref, ref, wsend.at[t - 1, 0, a], wrecv.at[kind, t - 1, o, a], to_core).wait_recv()
 
     def relay_own(c, t):
         arrive(c, t, 0, 0)
+
+        @pl.when((t <= j) & (j < last))
+        def _():
+            onward(c, t, t + 1, above)
+
+        @pl.when((t > j) & (j > 0))
+        def _():
+            onward(c, t, t - 1, below)
+
         send(c, t, 0, 1, 0, 1, to_x)
         send(c, t, 0, 2, 0, 2, to_y)
         send(c, t, 0, 4, 1, 0, to_core)
@@ -485,16 +556,29 @@
                 arrive(1 - c, t, o, 1)
 
     def drain(c):
+        @pl.when(j < last)
+        def _():
+            for copy in own_copies(c, True):
+                copy.wait_send()
+
+        @pl.when(j > 0)
+        def _():
+            for copy in own_copies(c, False):
+                copy.wait_send()
+
+        def sent(t, slot):
+            for a, ref in enumerate(piece_from(c, t, 0)):
+                remote(ref, ref, wsend.at[t - 1, slot, a], wrecv.at[0, t - 1, 0, a], to_core).wait_send()
+
         for t in range(1, n_tgt):
-            for slot in range(8):
-                for a, ref in enumerate(piece_from(c, t, 0)):
-                    remote(ref, ref, wsend.at[t - 1, slot, a], wrecv.at[0, t - 1, 0, a], to_core).wait_send()
+            pl.when(((t <= j) & (j < last)) | ((t > j) & (j > 0)))(functools.partial(sent, t, 0))
+            for slot in range(1, 8):
+                sent(t, slot)
 
     def by_core(function, *args):
         for c in range(2):
             pl.when(core == c)(functools.partial(function, c, *args))
 
-    order = [1, n_tgt - 1] + list(range(2, n_tgt - 1))
     feat_own = feat_all.at[pl.ds(pl.multiple_of(j * PAD, PAD), PAD), :]
     feat_sends = [
         remote(feat_own, feat_own, fsend.at[t - 1], frecv.at[t - 1], z_peers[t - 1]) for t in range(1, n_tgt)
@@ -503,6 +587,8 @@
         copy.start()
     by_core(start_z)
 
+    for name in ("to_grid", "ffn", "up", "from_grid_t", "gout", "down", "to_grid_t"):
+        staged[name].wait()
     grid_in = mm(to_grid[...], ffn[...]).astype(bf)
     pre = mm(grid_in, up[...])
     value = mm(from_grid_t[...], gout[...]).astype(bf)
@@ -521,36 +607,44 @@
 
     by_core(relay_own, order[0])
 
+    for name in ("esrc", "etgt", "eang", "wig"):
+        staged[name].wait()
     def iota(shape, axis):
         return lax.broadcasted_iota(jnp.int32, shape, axis)
 
     eye = (iota((slots, slots), 0) == iota((slots, slots), 1)).astype(bf)
+    n_s = n_tgt * PAD
+    live = iota((1, slots), 1) < count[...]
+
+    def pick_t(groups, ids):
+        index = iota((groups * angles, slots), 0)
+        return (index // angles == ids) & (index % angles == eang[...])
+
     pick_angle_t = (iota((angles, slots), 0) == eang[...]).astype(bf)
-    n_s, n_t = n_tgt * PAD, n_src * PAD
-    live = iota((1, slots), 1) < count[...]
-    mask_s_t = ((iota((n_s, slots), 0) // PAD == esrc[...]) & live).astype(bf)
-    mask_t_t = (iota((n_t, slots), 0) // PAD == etgt[...]).astype(bf)
-    pick_angle = mm_nt(eye, pick_angle_t).astype(bf)
-    mask_s = mm_nt(eye, mask_s_t).astype(bf)
-    mask_t = mm_nt(eye, mask_t_t).astype(bf)
-    spread_s = (iota((coef, n_s), 1) % PAD == iota((coef, n_s), 0)).astype(bf)
-    spread_t = (iota((coef, n_t), 1) % PAD == iota((coef, n_t), 0)).astype(bf)
+    pick_s_t = (pick_t(n_tgt, esrc[...]) & live).astype(bf)
+    pick_s = mm_nt(eye, pick_s_t).astype(bf)
+    pick_g = mm_nt(eye, pick_t(n_src, etgt[...]).astype(bf)).astype(bf)
+    mask_s_t = (iota((n_s, slots), 0) // PAD == esrc[...]) & live
     spread_s_t = (iota((n_s, coef), 0) % PAD == iota((n_s, coef), 1)).astype(bf)
-
-    by_core(relay_own, order[1])
-    for r in range(kept):
-        wide = mm_nt(spread_s_t, wig[r]).astype(bf)
-        xs_t[:, r * slots : (r + 1) * slots] = mm(wide, pick_angle_t).astype(bf) * mask_s_t
-    for t in range(2, n_tgt - 1):
-        by_core(relay_own, t)
+    wig_all = wig[...].reshape(kept * angles, coef)
 
     for copy in feat_sends:
         copy.wait_recv()
-    feats = feat_all[...]
+    for n in range(n_tgt):
+        table_s[n] = mm(wig_all, feat_all[n * PAD : n * PAD + coef, :]).astype(bf)
+    by_core(relay_own, order[1])
+    for copy in targ_sends:
+        copy.wait_recv()
+    for n in range(n_src):
+        table_t[n] = mm(wig_all, targ_all[n * PAD : n * PAD + coef, :]).astype(bf)
+        if n == n_src // 2:
+            by_core(relay, order[0])
+
+    by_core(relay_own, order[2])
     degree_cut = [7, 13, 19, 24, 29]
     for r in range(kept):
-        turn = mm(mm(pick_angle, wig[r]).astype(bf), spread_s).astype(bf) * mask_s
-        row = mm(turn, feats).astype(bf)
+        cut = slice(r * angles, (r + 1) * angles)
+        row = mm(pick_s, jnp.concatenate([table_s[n, cut, :] for n in range(n_tgt)], axis=0)).astype(bf)
         if r < degree_cut[0]:
             z0[:, r * channels : (r + 1) * channels] = row
         elif r < degree_cut[2]:
@@ -559,27 +653,24 @@
         else:
             p, at = divmod(r - degree_cut[2], 5)
             z2[p * slots : (p + 1) * slots, at * channels : (at + 1) * channels] = row
-    by_core(relay, order[0])
-
-    for copy in targ_sends:
-        copy.wait_recv()
-    targets = targ_all[...]
+    by_core(relay, order[1])
+    by_core(relay_diag, order[0])
     for r in range(kept):
-        turn = mm(mm(pick_angle, wig[r]).astype(bf), spread_t).astype(bf) * mask_t
-        grad_o[r] = mm(turn, targets) * message_scale
-        if r == 9:
-            by_core(relay, order[1])
-        if r == 19:
-            by_core(relay_diag, order[0])
-    for t in range(2, n_tgt - 1):
-        by_core(relay, t)
+        cut = slice(r * angles, (r + 1) * angles)
+        rows = jnp.concatenate([table_t[n, cut, :] for n in range(n_src)], axis=0)
+        grad_o[r] = mm(pick_g, rows) * message_scale
+    by_core(relay, order[2])
     by_core(relay_diag, order[1])
-    for t in range(2, n_tgt - 1):
-        by_core(relay_diag, t)
+    for r in range(kept):
+        wide = mm_nt(spread_s_t, wig[r]).astype(bf)
+        turned = mm(wide, pick_angle_t)
+        xs_t[:, r * slots : (r + 1) * slots] = jnp.where(mask_s_t, turned, 0.0).astype(bf)
+    by_core(relay_diag, order[2])
     for copy in locals_:
         copy.wait()
     by_core(finish)
 
+    staged["radial"].wait()
     gain = radial[...].astype(f32)
     h0 = mm(z0[...], w0[...])
     for r in range(8):
@@ -678,14 +769,33 @@
     bf, f32 = jnp.bfloat16, jnp.float32
     k0, k1, k2 = so2_zero.shape[0] * n_tgt, so2_one.shape[1] * n_tgt, so2_two.shape[1] * n_tgt
     vmem = pl.BlockSpec(memory_space=pltpu.VMEM)
-    hbm = pl.BlockSpec(memory_space=pl.ANY)
+    hbm = pl.BlockSpec(memory_space=pltpu.HBM)
     dma = pltpu.SemaphoreType.DMA
+    first = [
+        to_grid,
+        from_grid_t,
+        to_grid_t,
+        feat_in.reshape(coef, channels),
+        ffn_in.reshape(coef, channels),
+        grad_out.reshape(coef, channels),
+        ffn_up,
+        ffn_down,
+    ]
+    second = [
+        wigner.transpose(1, 0, 2),
+        edge_src.reshape(1, slots),
+        edge_tgt.reshape(1, slots),
+        edge_angle.reshape(1, slots),
+        edge_radial.reshape(slots, channels),
+    ]
     result = pl.pallas_call(
         functools.partial(fused_kernel, n_src, n_tgt),
         out_shape=jax.ShapeDtypeStruct((coef, channels), bf),
-        in_specs=[vmem] * 8 + [hbm] * 3 + [vmem] * 6,
+        in_specs=[hbm] * 16 + [vmem],
         out_specs=vmem,
-        scratch_shapes=[
+        scratch_shapes=[pltpu.VMEM(x.shape, x.dtype) for x in first + second]
+        + [
+            dma((len(first + second),)),
             pltpu.VMEM((k0, so2_zero.shape[1]), bf),
             pltpu.VMEM((2, k1, so2_one.shape[2]), bf),
             pltpu.VMEM((2, k2, so2_two.shape[2]), bf),
@@ -693,6 +803,8 @@
             pltpu.VMEM((n_src * PAD, channels), bf),
             pltpu.VMEM((n_tgt * PAD, channels), f32),
             pltpu.VMEM((n_tgt - 1, PAD, channels), f32),
+            pltpu.VMEM((n_tgt, kept * wigner.shape[0], channels), bf),
+            pltpu.VMEM((n_src, kept * wigner.shape[0], channels), bf),
             pltpu.VMEM((n_tgt * PAD, kept * slots), bf),
             pltpu.VMEM((slots, k0), bf),
             pltpu.VMEM((2 * slots, k1), bf),
@@ -702,6 +814,7 @@
             pltpu.VMEM((slots, so2_zero.shape[1]), bf),
             pltpu.VMEM((2 * slots, k1), bf),
             pltpu.VMEM((2 * slots, k2), bf),
+            dma((2, 2)),
             dma((n_tgt - 1, 8, 2)),
             dma((2, n_tgt - 1, 4, 2)),
             dma((3,)),
@@ -716,29 +829,18 @@
             collective_id=0, has_side_effects=True, vmem_limit_bytes=48 * 1024 * 1024
         ),
     )(
-        to_grid,
-        from_grid_t,
-        to_grid_t,
-        feat_in.reshape(coef, channels),
-        ffn_in.reshape(coef, channels),
-        grad_out.reshape(coef, channels),
-        ffn_up,
-        ffn_down,
+        *first,
         so2_zero,
         so2_one,
         so2_two,
-        wigner.transpose(1, 0, 2),
-        edge_src.reshape(1, slots),
-        edge_tgt.reshape(1, slots),
-        edge_angle.reshape(1, slots),
-        edge_radial.reshape(slots, channels),
+        *second,
         edge_count,
     )
     return result.reshape(feat_in.shape)
 
 
 def choose(*args):
-    if plan_fits(lax.axis_size("src"), *args[5:8]):
+    if plan_fits(lax.axis_size("src"), lax.axis_size("tgt"), *args[5:8]):
         return fused_on_device(*args)
     return on_device(*args)
 

time: 62.6 us -> 56.8 us (0.907)
  Pallas kernels: 52 us -> 46.1 us
    pallas_call x1, Pallas kernels: 52 us -> 46.1 us  [fused_on_device(): pl.pallas_call(functools.partial(fused_kernel, n_src, n_tgt), out_shape=j...]
where the time goes in v2:
time: 56.8 us; the launch traced here: 56.2 us
  Pallas kernels  46.1 us (81%)
  local copies, waits for them, and re-layouts  9.29 us (16%)
  between operations  0.81 us (1%)
    pallas_call x1, Pallas kernels, fused_on_device(): pl.pallas_call(functools.partial(fused_kernel, n_src, n_tgt), out_shape=j...  46.1 us
    unnamed x32, local copies, waits for them, and re-layouts  9.29 us

profile of v2, /device:TPU:0, one launch (start us, length us, event | category | flops | bytes accessed | tf_op | source)
XLA Modules:
  0.0 56.2 jit_solution(3113784852442497868)
XLA Ops:
  0.0 0.0 copy-start
  0.7 0.0 copy-start.3
  0.7 0.0 copy-start.4
  0.7 0.0 copy-start.7
  0.7 1.5 %copy.17 = bf16[64,29,49]{2,0,1:T(8,128)(2,1)S(1)} copy(bf16[64,29,49]{0,1,2:T(8,128)(2,1)} %param.24) | data formatting | bytes 363776 | tf_op args[8]
  2.3 0.0 copy-start.12
  2.3 0.0 copy-start.13
  2.3 0.0 copy-start.14
  2.3 0.0 copy-done
  2.3 0.0 copy-done.3
  2.3 0.0 copy-done.4
  2.3 0.0 copy-done.7
  2.3 0.6 %copy-done.12 = s32[1,1,128]{2,1,0:T(1,128)S(1)} copy-done((s32[1,1,128]{2,1,0:T(1,128)S(1)}, s32[1,1,128]{2,1,0:T(1,128)}, u32[]{:S(2)}) %copy-start.12) | copy-done | bytes 536
  2.9 0.0 copy-done.13
  2.9 0.0 copy-done.14
  3.0 0.0 copy-start.1
  3.0 1.0 %copy-done.1 = bf16[224,1024]{1,0:T(8,128)(2,1)S(1)} copy-done((bf16[224,1024]{1,0:T(8,128)(2,1)S(1)}, bf16[224,1024]{1,0:T(8,128)(2,1)}, u32[]{:S(2)}) %copy-start.1) | copy-done | bytes 458776
  4.0 0.0 copy-start.2
  4.0 1.0 %copy-done.2 = bf16[2,160,640]{2,1,0:T(8,128)(2,1)S(1)} copy-done((bf16[2,160,640]{2,1,0:T(8,128)(2,1)S(1)}, bf16[2,160,640]{2,1,0:T(8,128)(2,1)}, u32[]{:S(2)}) %copy-start.2) | copy-done | bytes 409624
  5.0 0.0 copy-start.5
  5.0 0.8 %copy-done.5 = bf16[208,49]{1,0:T(8,128)(2,1)S(1)} copy-done((bf16[208,49]{1,0:T(8,128)(2,1)S(1)}, bf16[208,49]{1,0:T(8,128)(2,1)}, u32[]{:S(2)}) %copy-start.5) | copy-done | bytes 20408
  5.8 0.0 copy-start.6
  5.8 0.8 %copy-done.6 = bf16[208,49]{1,0:T(8,128)(2,1)S(1)} copy-done((bf16[208,49]{1,0:T(8,128)(2,1)S(1)}, bf16[208,49]{1,0:T(8,128)(2,1)}, u32[]{:S(2)}) %copy-start.6) | copy-done | bytes 20408
  6.6 0.0 copy-start.8
  6.6 0.8 %copy-done.8 = bf16[64,208]{1,0:T(8,128)(2,1)S(1)} copy-done((bf16[64,208]{1,0:T(8,128)(2,1)S(1)}, bf16[64,208]{1,0:T(8,128)(2,1)}, u32[]{:S(2)}) %copy-start.8) | copy-done | bytes 26648
  7.4 0.0 copy-start.9
  7.4 0.7 %copy-done.9 = bf16[1,49,128]{2,1,0:T(8,128)(2,1)S(1)} copy-done((bf16[1,49,128]{2,1,0:T(8,128)(2,1)S(1)}, bf16[1,49,128]{2,1,0:T(8,128)(2,1)}, u32[]{:S(2)}) %copy-start.9) | copy-done | bytes 12568
  8.1 0.0 copy-start.10
  8.1 0.7 %copy-done.10 = bf16[1,49,128]{2,1,0:T(8,128)(2,1)S(1)} copy-done((bf16[1,49,128]{2,1,0:T(8,128)(2,1)S(1)}, bf16[1,49,128]{2,1,0:T(8,128)(2,1)}, u32[]{:S(2)}) %copy-start.10) | copy-done | bytes 12568
  8.8 0.0 copy-start.11
  8.8 0.7 %copy-done.11 = bf16[1,49,128]{2,1,0:T(8,128)(2,1)S(1)} copy-done((bf16[1,49,128]{2,1,0:T(8,128)(2,1)S(1)}, bf16[1,49,128]{2,1,0:T(8,128)(2,1)}, u32[]{:S(2)}) %copy-start.11) | copy-done | bytes 12568
  9.5 46.1 %shard_map.154 = bf16[49,128]{1,0:T(8,128)(2,1)S(1)} custom-call(bf16[208,49]{1,0:T(8,128)(2,1)S(1)} %copy-done.6, bf16[208,49]{1,0:T(8,128)(2,1)S(1)} %copy-done.5, bf16[64,208]{1,0:T(8,128)(2,1)S(1)} %copy-done.8, bf16[49,128]{1,0:T(8,128)(2,1)S(1)} %bitcast.12, bf16[49,128]{1,0:T(8,128)(2,1)S(1)} %bitcast.13, bf16[49,128]{1,0:T(8,128)(2,1)S(1)} %bitcast.14, ...), custom_call_target="tpu_custom_call" | custom-call | tf_op jit(solution)/shard_map/pallas_call | solution.py:791
  55.6 0.6 %copy.20 = bf16[1,49,128]{2,1,0:T(8,128)(2,1)} copy(bf16[1,49,128]{2,1,0:T(8,128)(2,1)S(1)} %bitcast.10) | data formatting | bytes 25088
Async XLA Ops:
  0.0 2.3 %copy-start = (bf16[2,192,768]{2,1,0:T(8,128)(2,1)S(1)}, bf16[2,192,768]{2,1,0:T(8,128)(2,1)}, u32[]{:S(2)}) copy-start(bf16[2,192,768]{2,1,0:T(8,128)(2,1)} %w1_in.1) | copy-start | bytes 1769476
  0.7 1.6 %copy-start.3 = (bf16[128,512]{1,0:T(8,128)(2,1)S(1)}, bf16[128,512]{1,0:T(8,128)(2,1)}, u32[]{:S(2)}) copy-start(bf16[128,512]{1,0:T(8,128)(2,1)} %up_in.1) | copy-start | bytes 393220
  0.7 1.6 %copy-start.4 = (bf16[512,128]{1,0:T(8,128)(2,1)S(1)}, bf16[512,128]{1,0:T(8,128)(2,1)}, u32[]{:S(2)}) copy-start(bf16[512,128]{1,0:T(8,128)(2,1)} %down_in.1) | copy-start | bytes 393220
  0.7 1.6 %copy-start.7 = (bf16[1,1,128,128]{3,2,1,0:T(8,128)(2,1)S(1)}, bf16[1,1,128,128]{3,2,1,0:T(8,128)(2,1)}, u32[]{:S(2)}) copy-start(bf16[1,1,128,128]{3,2,1,0:T(8,128)(2,1)} %param.28) | copy-start | bytes 98308
  2.3 0.7 %copy-start.12 = (s32[1,1,128]{2,1,0:T(1,128)S(1)}, s32[1,1,128]{2,1,0:T(1,128)}, u32[]{:S(2)}) copy-start(s32[1,1,128]{2,1,0:T(1,128)} %param.25) | copy-start | bytes 1540
  2.3 0.7 %copy-start.13 = (s32[1,1,128]{2,1,0:T(1,128)S(1)}, s32[1,1,128]{2,1,0:T(1,128)}, u32[]{:S(2)}) copy-start(s32[1,1,128]{2,1,0:T(1,128)} %param.26) | copy-start | bytes 1540
  2.3 0.7 %copy-start.14 = (s32[1,1,128]{2,1,0:T(1,128)S(1)}, s32[1,1,128]{2,1,0:T(1,128)}, u32[]{:S(2)}) copy-start(s32[1,1,128]{2,1,0:T(1,128)} %param.27) | copy-start | bytes 1540
  3.0 1.0 %copy-start.1 = (bf16[224,1024]{1,0:T(8,128)(2,1)S(1)}, bf16[224,1024]{1,0:T(8,128)(2,1)}, u32[]{:S(2)}) copy-start(bf16[224,1024]{1,0:T(8,128)(2,1)} %w0_in.1) | copy-start | bytes 1376260
  4.0 1.0 %copy-start.2 = (bf16[2,160,640]{2,1,0:T(8,128)(2,1)S(1)}, bf16[2,160,640]{2,1,0:T(8,128)(2,1)}, u32[]{:S(2)}) copy-start(bf16[2,160,640]{2,1,0:T(8,128)(2,1)} %w2_in.1) | copy-start | bytes 1228804
  5.0 0.8 %copy-start.5 = (bf16[208,49]{1,0:T(8,128)(2,1)S(1)}, bf16[208,49]{1,0:T(8,128)(2,1)}, u32[]{:S(2)}) copy-start(bf16[208,49]{1,0:T(8,128)(2,1)} %constant.27.from_grid_t_in) | copy-start | bytes 61156
  5.8 0.8 %copy-start.6 = (bf16[208,49]{1,0:T(8,128)(2,1)S(1)}, bf16[208,49]{1,0:T(8,128)(2,1)}, u32[]{:S(2)}) copy-start(bf16[208,49]{1,0:T(8,128)(2,1)} %constant.24.to_grid_in) | copy-start | bytes 61156
  6.6 0.8 %copy-start.8 = (bf16[64,208]{1,0:T(8,128)(2,1)S(1)}, bf16[64,208]{1,0:T(8,128)(2,1)}, u32[]{:S(2)}) copy-start(bf16[64,208]{1,0:T(8,128)(2,1)} %constant.29.to_grid_t_in) | copy-start | bytes 79876
  7.4 0.7 %copy-start.9 = (bf16[1,49,128]{2,1,0:T(8,128)(2,1)S(1)}, bf16[1,49,128]{2,1,0:T(8,128)(2,1)}, u32[]{:S(2)}) copy-start(bf16[1,49,128]{2,1,0:T(8,128)(2,1)} %param.16) | copy-start | bytes 37636
  8.1 0.7 %copy-start.10 = (bf16[1,49,128]{2,1,0:T(8,128)(2,1)S(1)}, bf16[1,49,128]{2,1,0:T(8,128)(2,1)}, u32[]{:S(2)}) copy-start(bf16[1,49,128]{2,1,0:T(8,128)(2,1)} %param.17) | copy-start | bytes 37636
  8.8 0.7 %copy-start.11 = (bf16[1,49,128]{2,1,0:T(8,128)(2,1)S(1)}, bf16[1,49,128]{2,1,0:T(8,128)(2,1)}, u32[]{:S(2)}) copy-start(bf16[1,49,128]{2,1,0:T(8,128)(2,1)} %param.18) | copy-start | bytes 37636

commit v3 on v2

--- a/solution.py
+++ b/solution.py
@@ -826,7 +826,7 @@
             dma((n_tgt - 1,)),
         ],
         compiler_params=pltpu.CompilerParams(
-            collective_id=0, has_side_effects=True, vmem_limit_bytes=48 * 1024 * 1024
+            collective_id=0, has_side_effects=True, vmem_limit_bytes=63 * 1024 * 1024
         ),
     )(
         *first,

time: 56.8 us -> 50.2 us (0.88)
  local copies, waits for them, and re-layouts: 9.29 us -> 3.54 us
    unnamed x32 -> x2, local copies, waits for them, and re-layouts: 9.29 us -> 3.54 us
where the time goes in v3:
time: 50.2 us; the launch traced here: 49.9 us
  Pallas kernels  45.7 us (91%)
  local copies, waits for them, and re-layouts  3.54 us (7%)
  between operations  0.66 us (1%)
    pallas_call x1, Pallas kernels, fused_on_device(): pl.pallas_call(functools.partial(fused_kernel, n_src, n_tgt), out_shape=j...  45.7 us
    unnamed x2, local copies, waits for them, and re-layouts  3.54 us

profile of v3, /device:TPU:0, one launch (start us, length us, event | category | flops | bytes accessed | tf_op | source)
XLA Modules:
  0.0 49.9 jit_solution(5538912975749364933)
XLA Ops:
  0.7 2.2 %copy.17 = bf16[64,29,49]{2,0,1:T(8,128)(2,1)} copy(bf16[64,29,49]{0,1,2:T(8,128)(2,1)} %param.24) | data formatting | bytes 363776 | tf_op args[8]
  2.9 45.7 %shard_map.154 = bf16[49,128]{1,0:T(8,128)(2,1)} custom-call(bf16[208,49]{1,0:T(8,128)(2,1)} %constant.24.to_grid_in, bf16[208,49]{1,0:T(8,128)(2,1)} %constant.27.from_grid_t_in, bf16[64,208]{1,0:T(8,128)(2,1)} %constant.29.to_grid_t_in, bf16[49,128]{1,0:T(8,128)(2,1)} %bitcast.12, bf16[49,128]{1,0:T(8,128)(2,1)} %bitcast.13, bf16[49,128]{1,0:T(8,128)(2,1)} %bitcast.14, ...), custom_call_target="tpu_custom_call" | custom-call | tf_op jit(solution)/shard_map/pallas_call | solution.py:791
  48.6 1.3 %copy.20 = bf16[1,49,128]{2,1,0:T(8,128)(2,1)} copy(bf16[1,49,128]{2,1,0:T(8,128)(2,1)} %bitcast.10) | data formatting | bytes 25088
